TPU v7x, 512 devices: a whole 4x8x8 slice. The times are simulated.
512 devices in a mesh: ctx: 64 (over y_lo, z, core), head: 8 (over x, y_hi).
Axes of the slice: x: 4, y: 8 (y_hi: 2, y_lo: 4; y = y_hi * 4 + y_lo), z: 8, core: 2. Of those that a mesh axis runs over, the one named last changes fastest.
Arguments:
- queries: bfloat16 [8192, 8192], P('ctx', 'head'), may hold values from -8 to 8
- key_vector_rows: bfloat16 [8192, 1024], P('ctx', 'head'), may hold values from -8 to 8
- values: bfloat16 [8192, 1024], P('ctx', 'head'), may hold values from -6 to 6
- doc_lengths: int32 [128], replicated, may hold values from 1 to 4224, 8192 in all
Outputs:
- attended: bfloat16 [8192, 8192], P(('ctx', 'head'))
Inputs may be any that keep to these rules, and one draw needn't show every extreme that they name: `doc_lengths`: the 128 lengths sum to 8192, and one of them is exactly 4224.
All inputs are finite; a program needn't handle non-finite values.
Results may differ from a plain program's by a relative error of at most 0.0025.
Values may be sent and summed in bfloat16 or wider, within the bound.
A program may use at most 64 MiB of HBM per device.

v0:
```python
import math

import jax
import jax.numpy as jnp
from jax import lax
from jax.sharding import PartitionSpec as P

HEAD_SIZE = 128


def doc_numbers(doc_ends, positions):
    return jnp.sum((doc_ends[None, :] <= positions[:, None]).astype(jnp.int32), axis=1)


def attend(running, block_of_keys, block_of_values, key_pos, query_info):
    query_heads, query_pos, query_docs, doc_ends = query_info
    key_docs = doc_numbers(doc_ends, key_pos)
    allowed = (
        (key_docs[None, :] == query_docs[:, None])
        & (key_pos[None, :] <= query_pos[:, None])
        & (key_pos[None, :] >= 0)
    )
    kv_heads = query_heads.shape[1]

    def update(current):
        old_max, old_total, old_sum = current
        key_heads = block_of_keys.reshape(block_of_keys.shape[0], kv_heads, HEAD_SIZE)
        value_heads = block_of_values.reshape(block_of_values.shape[0], kv_heads, HEAD_SIZE)
        scores = jnp.einsum(
            "qhgd,khd->hgqk", query_heads, key_heads, preferred_element_type=jnp.float32
        ) * (1.0 / math.sqrt(HEAD_SIZE))
        masked = jnp.where(allowed[None, None], scores, -1e30)
        new_max = jnp.maximum(old_max, jnp.max(masked, axis=-1))
        weights = jnp.where(allowed[None, None], jnp.exp(masked - new_max[..., None]), 0.0)
        rescale = jnp.exp(old_max - new_max)
        new_total = old_total * rescale + jnp.sum(weights, axis=-1)
        new_sum = old_sum * rescale[..., None] + jnp.einsum(
            "hgqk,khd->hgqd",
            weights.astype(jnp.bfloat16),
            value_heads,
            preferred_element_type=jnp.float32,
        )
        return (new_max, new_total, new_sum)

    return lax.cond(jnp.any(allowed), update, lambda current: current, running)


def finish(running, row_count):
    summed = running[2] / running[1][..., None]
    return jnp.transpose(summed, (2, 0, 1, 3)).reshape(row_count, -1).astype(jnp.bfloat16)


def local(queries, key_vector_rows, values, doc_lengths):
    row_count = queries.shape[0]
    head_count = queries.shape[1] // HEAD_SIZE
    kv_heads = key_vector_rows.shape[1] // HEAD_SIZE
    query_group_width = head_count // kv_heads
    own_index = lax.axis_index("ctx")
    doc_ends = jnp.cumsum(doc_lengths)
    block_first = own_index * row_count
    local_pos = block_first + jnp.arange(row_count, dtype=jnp.int32)
    initial = (
        jnp.full((kv_heads, query_group_width, row_count), -1e30, jnp.float32),
        jnp.zeros((kv_heads, query_group_width, row_count), jnp.float32),
        jnp.zeros((kv_heads, query_group_width, row_count, HEAD_SIZE), jnp.float32),
    )
    query_info = (
        queries.reshape(row_count, kv_heads, query_group_width, HEAD_SIZE),
        local_pos,
        doc_numbers(doc_ends, local_pos),
        doc_ends,
    )
    piece_keys = lax.all_gather(key_vector_rows, "ctx", axis=0, tiled=True)
    piece_values = lax.all_gather(values, "ctx", axis=0, tiled=True)
    block_count = piece_keys.shape[0] // row_count

    def one_shard(shard_index, current):
        offset = shard_index * row_count
        block_of_keys = lax.dynamic_slice_in_dim(piece_keys, offset, row_count, 0)
        block_of_values = lax.dynamic_slice_in_dim(piece_values, offset, row_count, 0)
        key_pos = offset + jnp.arange(row_count, dtype=jnp.int32)
        return attend(current, block_of_keys, block_of_values, key_pos, query_info)

    running = lax.fori_loop(0, block_count, one_shard, initial)
    output = finish(running, row_count)
    return lax.all_to_all(output, "head", split_axis=0, concat_axis=1, tiled=True)


def solution(mesh):
    in_specs = (P("ctx", "head"), P("ctx", "head"), P("ctx", "head"), P())
    out_specs = P(("ctx", "head"), None)
    return jax.shard_map(local, mesh=mesh, in_specs=in_specs, out_specs=out_specs, check_vma=False)
```

profile of v0, /device:TPU:88, one launch (start us, length us, event | category | flops | bytes accessed | tf_op | source)
XLA Modules:
  0.0 454.3 jit_solution(7774628474176715688)
XLA Ops:
  10.6 117.2 %all-gather.3.cloned.1.call-done = bf16[8192,128]{1,0:T(8,128)(2,1)} async-done(((bf16[128,128]{1,0:T(8,128)(2,1)}), bf16[8192,128]{1,0:T(8,128)(2,1)}) %all-gather.3.cloned.1.call-update) | async-done | bytes 2097168 | tf_op jit(solution)/shard_map/all_gather | solution.py:73
  127.7 118.2 %all-gather.5.cloned.1.call-done = bf16[8192,128]{1,0:T(8,128)(2,1)} async-done(((bf16[128,128]{1,0:T(8,128)(2,1)}), bf16[8192,128]{1,0:T(8,128)(2,1)}) %all-gather.5.cloned.1.call-update) | async-done | bytes 2097168 | tf_op jit(solution)/shard_map/all_gather | solution.py:74
  246.0 181.0 %while.18 = (s32[]{:T(128)}, f32[1,8,128]{2,1,0:T(8,128)S(1)}, f32[1,8,128]{2,1,0:T(8,128)S(1)}, f32[1,8,128,128]{3,2,1,0:T(8,128)S(1)}, s32[128]{0:T(128)S(1)},...) while((s32[]{:T(128)}, f32[1,8,128]{2,1,0:T(8,128)S(1)}, ...), condition=%wide.region_9.10_spmd.clone, body=%wide.region_2.9_spmd.clone.sunk | while | flops 68685184 | bytes 3085365 | solution.py:84
  274.2 2.4 conditional.3
  278.1 2.4 conditional.3
  282.0 2.4 conditional.3
  283.1 1.2 fusion.3
  286.0 2.4 conditional.3
  289.9 2.4 conditional.3
  291.0 1.2 fusion.3
  293.9 2.4 conditional.3
  294.9 1.2 fusion.3
  297.8 2.4 conditional.3
  301.7 2.4 conditional.3
  302.8 1.2 fusion.3
  305.7 2.4 conditional.3
  309.6 2.4 conditional.3
  313.6 2.4 conditional.3
  314.6 1.2 fusion.3
  317.5 2.4 conditional.3
  321.4 2.4 conditional.3
  322.5 1.2 fusion.3
  325.4 2.4 conditional.3
  326.4 1.2 fusion.3
  329.3 2.4 conditional.3
  333.3 2.4 conditional.3
  334.3 1.2 fusion.3
  337.2 2.4 conditional.3
  341.1 2.4 conditional.3
  345.1 2.4 conditional.3
  346.1 1.2 fusion.3
  349.0 2.4 conditional.3
  353.0 2.4 conditional.3
  356.9 2.4 conditional.3
  358.0 1.2 fusion.3
  360.9 2.4 conditional.3
  364.8 2.4 conditional.3
  368.7 2.4 conditional.3
  372.7 2.4 conditional.3
  376.6 2.4 conditional.3
  380.6 2.4 conditional.3
  384.5 2.4 conditional.3
  388.4 2.4 conditional.3
  392.4 2.4 conditional.3
  396.3 2.4 conditional.3
  400.3 2.4 conditional.3
  404.2 2.4 conditional.3
  427.5 19.3 %all_to_all.16 = bf16[8,16,1024]{2,1,0:T(8,128)(2,1)S(1)} all-to-all(bf16[8,16,1024]{2,1,0:T(8,128)(2,1)S(1)} %convert_element_type.36), channel_id=1, replica_groups=mesh['ctx'=64,'head'=8] {'head'}, dimensions={0} | all-to-all | bytes 524288 | tf_op jit(solution)/shard_map/all_to_all | solution.py:86
  (498 shorter events, 132.6 us)
Async XLA Ops:
  6.5 121.2 %all-gather.3.cloned.1.call-start = ((), (), s32[]{:S(2)}) async-start(), calls=%async_computation.1 | async-start | bytes 2129920 | tf_op jit(solution)/shard_map/all_gather | solution.py:73
  7.3 238.7 %all-gather.5.cloned.1.call-start = ((), (), s32[]{:S(2)}) async-start(), calls=%async_computation.2 | async-start | bytes 2129920 | tf_op jit(solution)/shard_map/all_gather | solution.py:74
Sparse Core Ops, SparseCore 0:
  9.5 118.1 all-gather.2
  129.9 116.0 all-gather.4
where the time goes:
time: 460 us; the launch traced here: 454 us
  waiting for transfers between devices  237 us (52%)
  matrix products  74.8 us (16%)
  other arithmetic  64.7 us (14%)
  loops' own time  42 us (9%)
  blocking collectives  19.3 us (4%)
  between operations  13.5 us (3%)
    all_gather x1, waiting for transfers between devices, local(): piece_values = lax.all_gather(values, 'ctx', axis=0, tiled=True)  118 us
    all_gather x1, waiting for transfers between devices, local(): piece_keys = lax.all_gather(key_vector_rows, 'ctx', axis=0, tiled=True)  117 us
    reduce_or x64, other arithmetic, attend(): return lax.cond(jnp.any(allowed), update, lambda current: current, running)  48.3 us
    dot_general x34, matrix products, update(): jnp.einsum('hgqk,khd->hgqd', weights.astype(jnp.bfloat16), value_heads, p...  40.7 us
    another operation x1, loops' own time, local(): running = lax.fori_loop(0, block_count, one_shard, initial)  39.5 us
    dot_general x34, matrix products, update(): jnp.einsum('qhgd,khd->hgqk', query_heads, key_heads, preferred_element_ty...  34.1 us
    all_to_all x1, blocking collectives, local(): lax.all_to_all(output, 'head', split_axis=0, concat_axis=1, tiled=True)  19.3 us
    reduce_sum x65, other arithmetic, doc_numbers(): jnp.sum((doc_ends[None, :] <= positions[:, None]).astype(jnp.int32), axis=1)  11.1 us
  transfers between devices with their start and end apart: 2, of which 2 were waited for; matrix products, arithmetic and copies ran while one was open for 1% of the time, Pallas kernels for 0%

commit v1 on v0

v1 whole, which is shorter than its diff:
```python
import functools
import math

import jax
import jax.numpy as jnp
from jax import lax
from jax.experimental import pallas as pl
from jax.experimental.pallas import tpu as pltpu
from jax.sharding import PartitionSpec as P

HEAD = 128
BLOCK = 128
ROWS, RING, HEADS = 4, 8, 8
GROUP = 8
WINDOW = 33
CHUNK = 32
EXP2_SCALE = math.log2(math.e) / math.sqrt(HEAD)
BIG = 1e30
MESH = pl.DeviceIdType.MESH


def kernel(
    q_ref, k_ref, v_ref, len_ref, out_ref,
    kv, qs, acc, top, total, stage,
    send_sem, recv_sem, out_send, out_recv,
):
    own = lax.axis_index("ctx")
    head = lax.axis_index("head")
    row, z, core = own // 16, lax.rem(own // 2, RING), lax.rem(own, 2)

    def ring(step):
        return lax.rem(z + step + RING, RING)

    def block(r, zz):
        return (r * RING + zz) * 2 + core

    barrier = pltpu.get_barrier_semaphore()

    def greet(device):
        pl.semaphore_signal(barrier, inc=1, device_id=device, device_id_type=MESH)

    has_next, has_next2 = row < ROWS - 1, row < ROWS - 2
    has_prev, has_prev2 = row >= 1, row >= 2
    sends_far = (core == 1) & (own + WINDOW <= 63)
    takes_far = (core == 0) & (own >= WINDOW)
    for step in (1, -1, 2, -2):
        greet((block(row, ring(step)), head))
    greet((own + 1 - 2 * core, head))
    pl.when(has_prev)(lambda: greet((own - 16, head)))
    pl.when(has_prev2)(lambda: greet((own - 32, head)))
    pl.when(takes_far)(lambda: greet((own - WINDOW, head)))
    for i in range(1, HEADS):
        greet((own, lax.rem(head + i, HEADS)))

    kv[own, 0:BLOCK, :] = k_ref[...]
    kv[own, BLOCK:, :] = v_ref[...]
    pl.semaphore_wait(
        barrier,
        5 + HEADS - 1
        + has_next.astype(jnp.int32) + has_next2.astype(jnp.int32)
        + sends_far.astype(jnp.int32),
    )

    sent = []

    def copy(slot, device, index):
        return pltpu.make_async_remote_copy(
            src_ref=kv.at[slot], dst_ref=kv.at[slot],
            send_sem=send_sem.at[index], recv_sem=recv_sem.at[slot],
            device_id=(device, head), device_id_type=MESH,
        )

    def send(slot, device, when=None):
        index = len(sent)
        sent.append(when)
        if when is None:
            copy(slot, device, index).start()
        else:
            pl.when(when())(lambda: copy(slot, device, index).start())

    def arrived(slot, when=None):
        wait = lambda: copy(slot, own + 1 - 2 * core, 0).wait_recv()
        if when is None:
            wait()
        else:
            pl.when(when)(wait)

    sibling = own + 1 - 2 * core

    send(own, sibling, lambda: core == 0)
    for step in (1, -1):
        send(own, block(row, ring(step)))
    send(own, own + 16, lambda: has_next)
    send(own, own + 32, lambda: has_next2)
    for step in (2, -2):
        send(own, block(row, ring(step)))
    send(own, own + WINDOW, lambda: sends_far)

    lengths = jnp.broadcast_to(len_ref[...], (16, 128))
    upper = (
        lax.broadcasted_iota(jnp.int32, (128, 128), 0)
        <= lax.broadcasted_iota(jnp.int32, (128, 128), 1)
    ).astype(jnp.float32).astype(jnp.bfloat16)

    def running(part):
        return jnp.dot(
            part.astype(jnp.float32).astype(jnp.bfloat16), upper,
            preferred_element_type=jnp.float32,
        )

    ends = (128.0 * running(lengths >> 7) + running(lengths & 127))[0:1, :]
    starts = ends - len_ref[...].astype(jnp.float32)

    def member(first):
        t = (first + lax.broadcasted_iota(jnp.int32, (BLOCK, 128), 0)).astype(jnp.float32)
        return (t >= starts) & (t < ends)

    other = jnp.where(member(own * BLOCK), 0.0, -BIG).astype(jnp.bfloat16)
    for c in range(BLOCK // CHUNK):
        for g in range(GROUP):
            at = c * CHUNK * GROUP + g * CHUNK
            qs[at:at + CHUNK, 0:HEAD] = q_ref[c * CHUNK:(c + 1) * CHUNK, g * HEAD:(g + 1) * HEAD]
            qs[at:at + CHUNK, HEAD:] = other[c * CHUNK:(c + 1) * CHUNK, :]
    acc[...] = jnp.zeros_like(acc)
    total[...] = jnp.zeros_like(total)
    top[...] = jnp.full_like(top, -3e38)

    def attend(slots, skipped, diagonal):
        width = BLOCK * len(slots)
        keys = jnp.concatenate([kv[s, 0:BLOCK, :] for s in slots], axis=0)
        docs = jnp.concatenate(
            [
                jnp.maximum(jnp.where(member(s * BLOCK), 1.0, 0.0), k)
                for s, k in zip(slots, skipped, strict=True)
            ],
            axis=0,
        ).astype(jnp.bfloat16)
        keys = jnp.concatenate([keys, docs], axis=1)
        vals = jnp.concatenate([kv[s, BLOCK:, :] for s in slots], axis=0)
        vals = jnp.concatenate([vals, jnp.ones((width, 128), jnp.bfloat16)], axis=1)
        size = CHUNK * GROUP
        for c in range(BLOCK // CHUNK):
            at = slice(c * size, (c + 1) * size)
            score = lax.dot_general(
                qs[at, :], keys, (((1,), (1,)), ((), ())), preferred_element_type=jnp.float32
            )
            if diagonal:
                p = c * CHUNK + lax.rem(lax.broadcasted_iota(jnp.int32, (size, BLOCK), 0), CHUNK)
                t = lax.broadcasted_iota(jnp.int32, (size, BLOCK), 1)
                score = jnp.concatenate(
                    [jnp.where(t <= p, score[:, 0:BLOCK], -BIG), score[:, BLOCK:]], axis=1
                )
            old = top[at, :]
            new = jnp.maximum(old, jnp.max(score, axis=1, keepdims=True))
            top[at, :] = new
            rescale = jnp.exp2((old - new) * EXP2_SCALE)
            shift = jnp.concatenate([new * EXP2_SCALE] * len(slots), axis=1)
            weight = jnp.exp2(score * EXP2_SCALE - shift).astype(jnp.bfloat16)
            both = jnp.dot(weight, vals, preferred_element_type=jnp.float32)
            acc[at, :] = acc[at, :] * rescale + both[:, 0:HEAD]
            total[at, :] = total[at, :] * rescale + both[:, HEAD:]

    def take_row(step, relay):
        zz = ring(step)
        slot = block(row, zz)
        arrived(slot)
        for to in relay:
            send(slot, block(row, ring(to)))
        send(slot, own + 16, lambda: has_next)
        send(slot, sibling, lambda: ring(step) < z)

    def take_r1(step):
        slot = block(row - 1, ring(step))
        arrived(slot, has_prev)
        send(slot, sibling, lambda: has_prev)

    def take_r2(step):
        zz = ring(step)
        slot = block(row - 2, zz)
        needed = has_prev2 & (zz >= z)
        if step == -2:
            arrived(slot, needed | (has_prev2 & (zz == 5) & (z == 7)))
            send(slot, block(row, ring(1)), lambda: has_prev2 & (ring(-2) >= 5) & (ring(-2) >= ring(1)))
        else:
            arrived(slot, needed)
        if step == 0:
            send(slot, block(row, ring(-1)), lambda: has_prev2 & (z >= 1))
            send(slot, block(row, ring(1)), lambda: has_prev2 & (z == 7))
            send(slot, block(row, ring(-2)), lambda: has_prev2 & (z >= 2))
            send(slot, block(row, ring(2)), lambda: has_prev2 & (z >= 5))
        if step == 2:
            send(slot, block(row, ring(-1)), lambda: has_prev2 & (z <= 5) & (z >= 1))
            send(slot, block(row, ring(-2)), lambda: has_prev2 & (z <= 5) & (z >= 2))
        send(slot, sibling, lambda: has_prev2 & (ring(step) >= z))

    take_row(-1, ())
    take_row(1, ())
    take_r1(0)
    take_r2(0)
    take_row(-2, (1, 2))
    take_row(2, (-1,))

    arrived(own - 1, core == 1)
    arrived(own - WINDOW, takes_far)
    near = jnp.where(core == 1, own - 1, jnp.where(takes_far, own - WINDOW, own))
    attend([own, near], [0.0, jnp.where(near == own, 1.0, 0.0)], True)

    def one_step(s, carry):
        def second():
            for step in (-1, 1):
                take_r1(step)
                take_r2(step)

        def third():
            for step in (-2, 2):
                take_r1(step)
                take_r2(step)
            for step in (-3, 3, -4):
                take_row(step, ())

        def fourth():
            for step in (-3, 3, -4):
                take_r1(step)
                take_r2(step)

        pl.when(s == 1)(second)
        pl.when(s == 3)(third)
        pl.when(s == 5)(fourth)
        distance = (s + 1) // 2
        zz = lax.rem(z + RING + jnp.where(lax.rem(s, 2) == 1, -distance, distance), RING)
        in_row = zz < z
        valid = in_row | has_prev2
        first = jnp.where(in_row, block(row, zz), jnp.where(has_prev2, block(row - 2, zz), own))
        before = jnp.where(has_prev, block(row - 1, zz), own)

        def work():
            turn = 1 - 2 * core
            arrived(first + turn, valid)
            arrived(before + turn, has_prev)
            pair = jnp.where(valid, 1, 0)
            pair1 = jnp.where(has_prev, 1, 0)
            attend(
                [first, first + turn * pair, before, before + turn * pair1],
                [jnp.where(valid, 0.0, 1.0)] * 2 + [jnp.where(has_prev, 0.0, 1.0)] * 2,
                False,
            )

        pl.when(valid | has_prev)(work)
        return carry

    lax.fori_loop(0, 8, one_step, 0)

    size = CHUNK * GROUP
    for c in range(BLOCK // CHUNK):
        at = slice(c * size, (c + 1) * size)
        result = (acc[at, :] / total[at, :]).astype(jnp.bfloat16)
        for g in range(GROUP):
            stage[c * CHUNK:(c + 1) * CHUNK, g * HEAD:(g + 1) * HEAD] = result[g * CHUNK:(g + 1) * CHUNK, :]
    width, kept = GROUP * HEAD, BLOCK // HEADS

    def out_copy(i, source):
        to = lax.rem(head + i, HEADS)
        return pltpu.make_async_remote_copy(
            src_ref=stage.at[pl.ds(pl.multiple_of(to * kept, kept), kept), :],
            dst_ref=out_ref.at[:, pl.ds(pl.multiple_of(source * width, width), width)],
            send_sem=out_send.at[i], recv_sem=out_recv.at[source],
            device_id=(own, to), device_id_type=MESH,
        )

    for i in (5, 3, 7, 1, 4, 2, 6):
        out_copy(i, head).start()
    out_ref[:, pl.ds(pl.multiple_of(head * width, width), width)] = stage[
        pl.ds(pl.multiple_of(head * kept, kept), kept), :
    ]
    for index, when in enumerate(sent):
        done = lambda: copy(own, sibling, index).wait_send()
        if when is None:
            done()
        else:
            pl.when(when())(done)
    for i in range(1, HEADS):
        out_copy(i, lax.rem(head + i, HEADS)).wait_recv()
    for i in range(1, HEADS):
        out_copy(i, head).wait_send()


SENDS = 96


def local(queries, key_vector_rows, values, doc_lengths):
    vmem = pl.BlockSpec(memory_space=pltpu.VMEM)
    rows = BLOCK * GROUP
    return pl.pallas_call(
        kernel,
        out_shape=jax.ShapeDtypeStruct((BLOCK // HEADS, HEADS * GROUP * HEAD), jnp.bfloat16),
        in_specs=[vmem] * 4,
        out_specs=vmem,
        scratch_shapes=[
            pltpu.VMEM((64, 2 * BLOCK, HEAD), jnp.bfloat16),
            pltpu.VMEM((rows, 2 * HEAD), jnp.bfloat16),
            pltpu.VMEM((rows, HEAD), jnp.float32),
            pltpu.VMEM((rows, 128), jnp.float32),
            pltpu.VMEM((rows, 128), jnp.float32),
            pltpu.VMEM((BLOCK, GROUP * HEAD), jnp.bfloat16),
            pltpu.SemaphoreType.DMA((SENDS,)),
            pltpu.SemaphoreType.DMA((64,)),
            pltpu.SemaphoreType.DMA((HEADS,)),
            pltpu.SemaphoreType.DMA((HEADS,)),
        ],
        compiler_params=pltpu.CompilerParams(
            collective_id=0, has_side_effects=True, vmem_limit_bytes=32 << 20
        ),
        name="attention",
    )(queries, key_vector_rows, values, doc_lengths.reshape(1, 128))


def solution(mesh):
    in_specs = (P("ctx", "head"), P("ctx", "head"), P("ctx", "head"), P())
    out_specs = P(("ctx", "head"), None)
    return jax.shard_map(local, mesh=mesh, in_specs=in_specs, out_specs=out_specs, check_vma=False)
```

time: 460 us -> 52.8 us (0.11)
  the two profiles are of different devices: /device:TPU:88 before, /device:TPU:56 now
where the time goes in v1:
time: 52.8 us; the launch traced here: 52.5 us
  Pallas kernels  48.7 us (92%)
  local copies, waits for them, and re-layouts  3.82 us (7%)
    pallas_call x1, Pallas kernels, local(): pl.pallas_call(kernel, out_shape=jax.ShapeDtypeStruct((BLOCK // HEADS, HE...  48.7 us
    unnamed x9, local copies, waits for them, and re-layouts  3.82 us

profile of v1, /device:TPU:56, one launch (start us, length us, event | category | flops | bytes accessed | tf_op | source)
XLA Modules:
  0.0 52.5 jit_solution(13499250146757716916)
XLA Ops:
  0.0 0.0 copy-start.3
  0.0 0.7 %copy-done.3 = s32[128]{0:T(128)S(1)} copy-done((s32[128]{0:T(128)S(1)}, s32[128]{0:T(128)}, u32[]{:S(2)}) %copy-start.3) | copy-done | bytes 536
  0.7 0.0 copy-start
  0.7 0.9 %copy-done = bf16[128,1024]{1,0:T(8,128)(2,1)S(1)} copy-done((bf16[128,1024]{1,0:T(8,128)(2,1)S(1)}, bf16[128,1024]{1,0:T(8,128)(2,1)}, u32[]{:S(2)}) %copy-start) | copy-done | bytes 262168
  1.6 0.0 copy-start.1
  1.6 0.8 %copy-done.1 = bf16[128,128]{1,0:T(8,128)(2,1)S(1)} copy-done((bf16[128,128]{1,0:T(8,128)(2,1)S(1)}, bf16[128,128]{1,0:T(8,128)(2,1)}, u32[]{:S(2)}) %copy-start.1) | copy-done | bytes 32792
  2.4 0.0 copy-start.2
  2.4 0.8 %copy-done.2 = bf16[128,128]{1,0:T(8,128)(2,1)S(1)} copy-done((bf16[128,128]{1,0:T(8,128)(2,1)S(1)}, bf16[128,128]{1,0:T(8,128)(2,1)}, u32[]{:S(2)}) %copy-start.2) | copy-done | bytes 32792
  3.1 48.7 %attention.1 = bf16[16,8192]{1,0:T(8,128)(2,1)S(1)} custom-call(bf16[128,1024]{1,0:T(8,128)(2,1)S(1)} %copy-done, bf16[128,128]{1,0:T(8,128)(2,1)S(1)} %copy-done.1, bf16[128,128]{1,0:T(8,128)(2,1)S(1)} %copy-done.2, s32[1,128]{1,0:T(1,128)S(1)} %bitcast.1), custom_call_target="tpu_custom_call" | custom-call | tf_op jit(solution)/shard_map/attention/pallas_call | solution.py:293
  51.8 0.7 %copy.6 = bf16[16,8192]{1,0:T(8,128)(2,1)} copy(bf16[16,8192]{1,0:T(8,128)(2,1)S(1)} %attention.1) | data formatting | bytes 524288
Async XLA Ops:
  0.0 0.7 %copy-start.3 = (s32[128]{0:T(128)S(1)}, s32[128]{0:T(128)}, u32[]{:S(2)}) copy-start(s32[128]{0:T(128)} %param.7) | copy-start | bytes 1540
  0.7 0.9 %copy-start = (bf16[128,1024]{1,0:T(8,128)(2,1)S(1)}, bf16[128,1024]{1,0:T(8,128)(2,1)}, u32[]{:S(2)}) copy-start(bf16[128,1024]{1,0:T(8,128)(2,1)} %q_ref.1) | copy-start | bytes 786436
  1.6 0.8 %copy-start.1 = (bf16[128,128]{1,0:T(8,128)(2,1)S(1)}, bf16[128,128]{1,0:T(8,128)(2,1)}, u32[]{:S(2)}) copy-start(bf16[128,128]{1,0:T(8,128)(2,1)} %k_ref.1) | copy-start | bytes 98308
  2.4 0.8 %copy-start.2 = (bf16[128,128]{1,0:T(8,128)(2,1)S(1)}, bf16[128,128]{1,0:T(8,128)(2,1)}, u32[]{:S(2)}) copy-start(bf16[128,128]{1,0:T(8,128)(2,1)} %v_ref.1) | copy-start | bytes 98308

commit v2 on v1

v2 whole, which is shorter than its diff:
```python
import functools
import math

import jax
import jax.numpy as jnp
from jax import lax
from jax.experimental import pallas as pl
from jax.experimental.pallas import tpu as pltpu
from jax.sharding import PartitionSpec as P

HEAD = 128
BLOCK = 128
ROWS, RING, HEADS = 4, 8, 8
GROUP = 8
WINDOW = 33
CHUNK = 32
EXP2_SCALE = math.log2(math.e) / math.sqrt(HEAD)
BIG = 1e30
MESH = pl.DeviceIdType.MESH
STEPS = (0, -1, 1, -2, 2, -3, 3, 4)


def kernel(
    q_hbm, k_hbm, v_hbm, len_hbm, out_ref,
    q_ref, len_ref, kv, qs, acc, top, total, stage,
    load_sem, send_sem, recv_sem, out_send, out_recv, out_sem,
):
    own = lax.axis_index("ctx")
    head = lax.axis_index("head")
    row, z, core = own // 16, lax.rem(own // 2, RING), lax.rem(own, 2)
    sibling = own + 1 - 2 * core

    loads = [
        pltpu.make_async_copy(k_hbm, kv.at[own, pl.ds(0, BLOCK), :], load_sem.at[0]),
        pltpu.make_async_copy(v_hbm, kv.at[own, pl.ds(BLOCK, BLOCK), :], load_sem.at[1]),
        pltpu.make_async_copy(len_hbm, len_ref, load_sem.at[2]),
        pltpu.make_async_copy(q_hbm, q_ref, load_sem.at[3]),
    ]
    for load in loads:
        load.start()

    def block(r, zz):
        return (r * RING + zz) * 2 + core

    def chip(step):
        return block(row, lax.rem(z + step + RING, RING))

    def pick(table, index):
        return sum(jnp.where(index == i, entry, 0) for i, entry in enumerate(table))

    turns = [lax.rem(z + step + RING, RING) for step in STEPS]

    def number(flag):
        return flag.astype(jnp.int32)

    has_next, has_next2 = row < ROWS - 1, row < ROWS - 2
    has_prev, has_prev2 = row >= 1, row >= 2
    far_sender = (core == 1) & (own + WINDOW <= 63)
    far_taker = (core == 0) & (own >= WINDOW)
    rank = lax.rem(head, 2) * 4 + head // 2

    def by_rank(i):
        other = lax.rem(rank + i, HEADS)
        return other, lax.rem(other, 4) * 2 + other // 4

    barrier = pltpu.get_barrier_semaphore()

    def signal(sem, ctx, hd=None):
        pl.semaphore_signal(
            sem, inc=1, device_id=(ctx, head if hd is None else hd), device_id_type=MESH
        )

    steps = (1, -1, 2, -2)
    for step in steps:
        signal(barrier, chip(step))
    pl.when(has_prev)(lambda: signal(barrier, own - 16))
    pl.when(has_prev2)(lambda: signal(barrier, own - 32))
    signal(barrier, sibling)

    pl.when(far_taker)(lambda: signal(barrier, own - WINDOW))
    for i in range(1, HEADS):
        other, hd = by_rank(i)
        pl.when(other > rank)(lambda hd=hd: signal(barrier, own, hd))
    pl.semaphore_wait(
        barrier,
        5 + rank + number(has_next) + number(has_next2) + number(far_sender),
    )

    def copy(slot, device, index):
        return pltpu.make_async_remote_copy(
            src_ref=kv.at[slot], dst_ref=kv.at[slot],
            send_sem=send_sem.at[index], recv_sem=recv_sem.at[slot],
            device_id=(device, head), device_id_type=MESH,
        )

    def send(slot, device, index, when):
        pl.when(when)(lambda: copy(slot, device, index).start())

    def arrived(slot, when):
        pl.when(when)(lambda: copy(slot, sibling, 0).wait_recv())

    def sent(index, when):
        pl.when(when)(lambda: copy(own, sibling, index).wait_send())

    def r0_plan(s):
        zs = pick(turns, s)
        e = lax.rem(z - zs + RING, RING)
        due = (e > 0) & (
            has_next | jnp.where(e <= 4, zs < z, jnp.where(e == 7, zs == 0, zs <= 2))
        )
        first, up, down = e == 0, due & (e == 2), due & (e == 6)
        to = (
            (first | up) & (has_next | ((zs <= z) & (z < 7))),
            (first & (has_next | (zs == 0))) | (down & (has_next | (zs <= 2))),
            (first | up) & (has_next | ((zs <= z) & (z < 6))),
            first & (has_next | (zs <= 2)),
        )
        return block(row, zs), due, to, zs < z

    def r1_slot(s):
        return block(row - 1, pick(turns, s))

    def r2_plan(s):
        zs = pick(turns, s)
        e = lax.rem(z - zs + RING, RING)
        due = has_prev2 & (
            (z <= zs) & ((e == 0) | (e >= 4)) | ((e == 1) & (zs == 7)) | ((e == 2) | (e == 3)) & (zs >= 5)
        )
        first, up, down = due & (e == 0), due & (e == 2), due & (e == 6)
        to = (
            (first & (z == 7)) | up,
            (first | down) & (z >= 1),
            first & (z >= 5),
            (first | down) & (z >= 2),
        )
        return block(row - 2, zs), due, to, has_prev2 & (zs >= z)

    loads[0].wait()
    loads[1].wait()

    def pass_on(base, slot, to):
        for k, step in enumerate(steps):
            send(slot, chip(step), base + k, to[k])

    _, _, to, _ = r0_plan(0)
    pass_on(0, own, to)
    send(own, own + 16, 4, has_next)
    send(own, own + 32, 48, has_next2)
    send(own, sibling, 5, core == 0)
    send(own, own + WINDOW, 49, far_sender)
    for i in range(1, HEADS):
        other, hd = by_rank(i)
        pl.when(other < rank)(lambda hd=hd: signal(out_sem, own, hd))

    loads[2].wait()
    lengths = jnp.broadcast_to(len_ref[...], (16, 128))
    upper = (
        lax.broadcasted_iota(jnp.int32, (128, 128), 0)
        <= lax.broadcasted_iota(jnp.int32, (128, 128), 1)
    ).astype(jnp.float32).astype(jnp.bfloat16)

    def running(part):
        return jnp.dot(
            part.astype(jnp.float32).astype(jnp.bfloat16), upper,
            preferred_element_type=jnp.float32,
        )

    ends = (128.0 * running(lengths >> 7) + running(lengths & 127))[0:1, :]
    starts = ends - len_ref[...].astype(jnp.float32)

    def member(first):
        t = (first + lax.broadcasted_iota(jnp.int32, (BLOCK, 128), 0)).astype(jnp.float32)
        return (t >= starts) & (t < ends)

    loads[3].wait()
    other = jnp.where(member(own * BLOCK), 0.0, -BIG).astype(jnp.bfloat16)
    for c in range(BLOCK // CHUNK):
        for g in range(GROUP):
            at = c * CHUNK * GROUP + g * CHUNK
            qs[at:at + CHUNK, 0:HEAD] = q_ref[c * CHUNK:(c + 1) * CHUNK, g * HEAD:(g + 1) * HEAD]
            qs[at:at + CHUNK, HEAD:] = other[c * CHUNK:(c + 1) * CHUNK, :]
    acc[...] = jnp.zeros_like(acc)
    total[...] = jnp.zeros_like(total)
    top[...] = jnp.full_like(top, -3e38)

    def attend(slots, skipped, diagonal):
        width = BLOCK * len(slots)
        keys = jnp.concatenate([kv[s, 0:BLOCK, :] for s in slots], axis=0)
        docs = jnp.concatenate(
            [
                jnp.maximum(jnp.where(member(s * BLOCK), 1.0, 0.0), k)
                for s, k in zip(slots, skipped, strict=True)
            ],
            axis=0,
        ).astype(jnp.bfloat16)
        keys = jnp.concatenate([keys, docs], axis=1)
        vals = jnp.concatenate([kv[s, BLOCK:, :] for s in slots], axis=0)
        vals = jnp.concatenate([vals, jnp.ones((width, 128), jnp.bfloat16)], axis=1)
        size = CHUNK * GROUP
        for c in range(BLOCK // CHUNK):
            at = slice(c * size, (c + 1) * size)
            score = lax.dot_general(
                qs[at, :], keys, (((1,), (1,)), ((), ())), preferred_element_type=jnp.float32
            )
            if diagonal:
                p = c * CHUNK + lax.rem(lax.broadcasted_iota(jnp.int32, (size, BLOCK), 0), CHUNK)
                t = lax.broadcasted_iota(jnp.int32, (size, BLOCK), 1)
                score = jnp.concatenate(
                    [jnp.where(t <= p, score[:, 0:BLOCK], -BIG), score[:, BLOCK:]], axis=1
                )
            old = top[at, :]
            new = jnp.maximum(old, jnp.max(score, axis=1, keepdims=True))
            top[at, :] = new
            rescale = jnp.exp2((old - new) * EXP2_SCALE)
            shift = jnp.concatenate([new * EXP2_SCALE] * len(slots), axis=1)
            weight = jnp.exp2(score * EXP2_SCALE - shift).astype(jnp.bfloat16)
            both = jnp.dot(weight, vals, preferred_element_type=jnp.float32)
            acc[at, :] = acc[at, :] * rescale + both[:, 0:HEAD]
            total[at, :] = total[at, :] * rescale + both[:, HEAD:]

    def r0(s):
        slot, due, to, wanted = r0_plan(s)
        arrived(slot, due)
        pass_on(s * 6, slot, to)
        send(slot, own + 16, s * 6 + 4, has_next)
        send(slot, sibling, s * 6 + 5, wanted)

    def r1(s):
        arrived(r1_slot(s), has_prev)
        send(r1_slot(s), sibling, 50 + s, has_prev)

    def r2(s):
        slot, due, to, wanted = r2_plan(s)
        arrived(slot, due)
        pass_on(58 + s * 5, slot, to)
        send(slot, sibling, 62 + s * 5, wanted)

    def own_step():
        arrived(own - 1, core == 1)
        arrived(own - WINDOW, far_taker)
        other = jnp.where(core == 1, own - 1, jnp.where(far_taker, own - WINDOW, own))
        attend([own, other], [0.0, jnp.where(other == own, 1.0, 0.0)], True)

    def take(*which):
        for plan, s in which:
            plan(s)

    take((r0, 1), (r0, 2), (r1, 0), (r2, 0), (r0, 3), (r0, 4))
    own_step()

    def one_step(s, carry):
        pl.when(s == 1)(lambda: take((r1, 1), (r2, 1), (r1, 2), (r2, 2)))
        pl.when(s == 3)(lambda: take((r1, 3), (r2, 3), (r1, 4), (r2, 4), (r0, 5), (r0, 6), (r0, 7)))
        pl.when(s >= 5)(lambda: take((r1, s), (r2, s)))
        zz = pick(turns, s)
        in_row = zz < z
        valid = in_row | has_prev2
        first = jnp.where(in_row, block(row, zz), jnp.where(has_prev2, block(row - 2, zz), own))
        prior = jnp.where(has_prev, block(row - 1, zz), own)

        def work():
            turn = 1 - 2 * core
            arrived(first + turn, valid)
            arrived(prior + turn, has_prev)
            attend(
                [first, first + turn * number(valid), prior, prior + turn * number(has_prev)],
                [jnp.where(valid, 0.0, 1.0)] * 2 + [jnp.where(has_prev, 0.0, 1.0)] * 2,
                False,
            )

        pl.when(valid | has_prev)(work)
        return carry

    lax.fori_loop(0, 8, one_step, 0)

    size = CHUNK * GROUP
    width, kept = GROUP * HEAD, BLOCK // HEADS

    def out_copy(to, source):
        return pltpu.make_async_remote_copy(
            src_ref=stage.at[pl.ds(to * kept, kept), :],
            dst_ref=out_ref.at[:, pl.ds(pl.multiple_of(source * width, width), width)],
            send_sem=out_send.at[to], recv_sem=out_recv.at[source],
            device_id=(own, to), device_id_type=MESH,
        )

    pl.when(rank < HEADS - 1)(lambda: pl.semaphore_wait(out_sem, HEADS - 1 - rank))
    for c in range(BLOCK // CHUNK):
        at = slice(c * size, (c + 1) * size)
        result = (acc[at, :] / total[at, :]).astype(jnp.bfloat16)
        for g in range(GROUP):
            stage[c * CHUNK:(c + 1) * CHUNK, g * HEAD:(g + 1) * HEAD] = result[g * CHUNK:(g + 1) * CHUNK, :]
        for to in (2 * c, 2 * c + 1):
            pl.when(head != to)(lambda to=to: out_copy(to, head).start())
    out_ref[:, pl.ds(pl.multiple_of(head * width, width), width)] = stage[
        pl.ds(pl.multiple_of(head * kept, kept), kept), :
    ]
    sent(48, has_next2)
    sent(49, far_sender)

    def finish(s, carry):
        _, _, to, wanted = r0_plan(s)
        for k in range(4):
            sent(s * 6 + k, to[k])
        sent(s * 6 + 4, has_next)
        sent(s * 6 + 5, jnp.where(s == 0, number(core == 0), number(wanted)) == 1)
        sent(50 + s, has_prev)
        _, _, to, wanted = r2_plan(s)
        for k in range(4):
            sent(58 + s * 5 + k, to[k])
        sent(62 + s * 5, wanted)
        return carry

    lax.fori_loop(0, RING, finish, 0)
    for other in range(HEADS):
        pl.when(head != other)(lambda other=other: out_copy(0, other).wait_recv())
    for to in range(HEADS):
        pl.when(head != to)(lambda to=to: out_copy(to, head).wait_send())


SENDS = 98


def local(queries, key_vector_rows, values, doc_lengths):
    rows = BLOCK * GROUP
    return pl.pallas_call(
        kernel,
        out_shape=pltpu.VMEM((BLOCK // HEADS, HEADS * GROUP * HEAD), jnp.bfloat16),
        in_specs=[pl.BlockSpec(memory_space=pltpu.HBM)] * 4,
        out_specs=pl.BlockSpec(memory_space=pltpu.VMEM),
        scratch_shapes=[
            pltpu.VMEM((BLOCK, GROUP * HEAD), jnp.bfloat16),
            pltpu.VMEM((1, 128), jnp.int32),
            pltpu.VMEM((64, 2 * BLOCK, HEAD), jnp.bfloat16),
            pltpu.VMEM((rows, 2 * HEAD), jnp.bfloat16),
            pltpu.VMEM((rows, HEAD), jnp.float32),
            pltpu.VMEM((rows, 128), jnp.float32),
            pltpu.VMEM((rows, 128), jnp.float32),
            pltpu.VMEM((BLOCK, GROUP * HEAD), jnp.bfloat16),
            pltpu.SemaphoreType.DMA((4,)),
            pltpu.SemaphoreType.DMA((SENDS,)),
            pltpu.SemaphoreType.DMA((64,)),
            pltpu.SemaphoreType.DMA((HEADS,)),
            pltpu.SemaphoreType.DMA((HEADS,)),
            pltpu.SemaphoreType.REGULAR,
        ],
        compiler_params=pltpu.CompilerParams(
            collective_id=0, has_side_effects=True, vmem_limit_bytes=55500 << 10
        ),
        name="attention",
    )(queries, key_vector_rows, values, doc_lengths.reshape(1, 128))


def solution(mesh):
    in_specs = (P("ctx", "head"), P("ctx", "head"), P("ctx", "head"), P())
    out_specs = P(("ctx", "head"), None)
    return jax.shard_map(local, mesh=mesh, in_specs=in_specs, out_specs=out_specs, check_vma=False)
```

time: 52.8 us -> 48 us (0.909)
  the two profiles are of different devices: /device:TPU:56 before, /device:TPU:30 now
where the time goes in v2:
time: 48 us; the launch traced here: 47.9 us
  Pallas kernels  47.2 us (98%)
  local copies, waits for them, and re-layouts  0.71 us (1%)
    pallas_call x1, Pallas kernels, local(): pl.pallas_call(kernel, out_shape=pltpu.VMEM((BLOCK // HEADS, HEADS * GROU...  47.2 us

profile of v2, /device:TPU:30, one launch (start us, length us, event | category | flops | bytes accessed | tf_op | source)
XLA Modules:
  0.0 47.9 jit_solution(13300901626181727191)
XLA Ops:
  0.0 47.2 %attention.1 = bf16[16,8192]{1,0:T(8,128)(2,1)S(1)} custom-call(bf16[128,1024]{1,0:T(8,128)(2,1)} %q_hbm.1, bf16[128,128]{1,0:T(8,128)(2,1)} %k_hbm.1, bf16[128,128]{1,0:T(8,128)(2,1)} %v_hbm.1, s32[1,128]{1,0:T(1,128)} %bitcast.1), custom_call_target="tpu_custom_call" | custom-call | tf_op jit(solution)/shard_map/attention/pallas_call | solution.py:326
  47.2 0.7 %copy.6 = bf16[16,8192]{1,0:T(8,128)(2,1)} copy(bf16[16,8192]{1,0:T(8,128)(2,1)S(1)} %attention.1) | data formatting | bytes 524288

commit v3 on v2

--- a/solution.py
+++ b/solution.py
@@ -70,7 +70,7 @@
             sem, inc=1, device_id=(ctx, head if hd is None else hd), device_id_type=MESH
         )
 
-    steps = (1, -1, 2, -2)
+    steps = (1, -1)
     for step in steps:
         signal(barrier, chip(step))
     pl.when(has_prev)(lambda: signal(barrier, own - 16))
@@ -83,7 +83,7 @@
         pl.when(other > rank)(lambda hd=hd: signal(barrier, own, hd))
     pl.semaphore_wait(
         barrier,
-        5 + rank + number(has_next) + number(has_next2) + number(far_sender),
+        3 + rank + number(has_next) + number(has_next2) + number(far_sender),
     )
 
     def copy(slot, device, index):
@@ -105,17 +105,10 @@
     def r0_plan(s):
         zs = pick(turns, s)
         e = lax.rem(z - zs + RING, RING)
-        due = (e > 0) & (
-            has_next | jnp.where(e <= 4, zs < z, jnp.where(e == 7, zs == 0, zs <= 2))
-        )
-        first, up, down = e == 0, due & (e == 2), due & (e == 6)
-        to = (
-            (first | up) & (has_next | ((zs <= z) & (z < 7))),
-            (first & (has_next | (zs == 0))) | (down & (has_next | (zs <= 2))),
-            (first | up) & (has_next | ((zs <= z) & (z < 6))),
-            first & (has_next | (zs <= 2)),
-        )
-        return block(row, zs), due, to, zs < z
+        due = (e > 0) & (has_next | jnp.where(e <= 4, zs < z, zs <= 2))
+        up = ((e == 0) | due) & (e <= 3) & (has_next | ((zs <= z) & (z < 7)))
+        down = ((e == 0) | (due & (e >= 6))) & (has_next | (zs <= 2))
+        return block(row, zs), due, (up, down), zs < z
 
     def r1_slot(s):
         return block(row - 1, pick(turns, s))
@@ -123,17 +116,10 @@
     def r2_plan(s):
         zs = pick(turns, s)
         e = lax.rem(z - zs + RING, RING)
-        due = has_prev2 & (
-            (z <= zs) & ((e == 0) | (e >= 4)) | ((e == 1) & (zs == 7)) | ((e == 2) | (e == 3)) & (zs >= 5)
-        )
-        first, up, down = due & (e == 0), due & (e == 2), due & (e == 6)
-        to = (
-            (first & (z == 7)) | up,
-            (first | down) & (z >= 1),
-            first & (z >= 5),
-            (first | down) & (z >= 2),
-        )
-        return block(row - 2, zs), due, to, has_prev2 & (zs >= z)
+        due = has_prev2 & ((e == 0) | jnp.where(e <= 4, zs >= 4, z < zs))
+        up = due & (e <= 3) & (zs >= 4)
+        down = due & ((e == 0) | (e >= 6)) & (z >= 1)
+        return block(row - 2, zs), due, (up, down), has_prev2 & (zs >= z)
 
     loads[0].wait()
     loads[1].wait()
@@ -245,13 +231,14 @@
         for plan, s in which:
             plan(s)
 
-    take((r0, 1), (r0, 2), (r1, 0), (r2, 0), (r0, 3), (r0, 4))
+    take((r0, 1), (r0, 2), (r2, 0), (r1, 0))
     own_step()
 
     def one_step(s, carry):
-        pl.when(s == 1)(lambda: take((r1, 1), (r2, 1), (r1, 2), (r2, 2)))
-        pl.when(s == 3)(lambda: take((r1, 3), (r2, 3), (r1, 4), (r2, 4), (r0, 5), (r0, 6), (r0, 7)))
-        pl.when(s >= 5)(lambda: take((r1, s), (r2, s)))
+        pl.when(s == 1)(lambda: take((r0, 3), (r0, 4), (r2, 1), (r2, 2), (r1, 1), (r1, 2)))
+        pl.when(s == 3)(lambda: take((r0, 5), (r0, 6), (r2, 3), (r2, 4), (r1, 3), (r1, 4)))
+        pl.when(s == 5)(lambda: take((r0, 7), (r2, 5), (r2, 6), (r1, 5), (r1, 6)))
+        pl.when(s == 7)(lambda: take((r2, 7), (r1, 7)))
         zz = pick(turns, s)
         in_row = zz < z
         valid = in_row | has_prev2
@@ -300,13 +287,13 @@
 
     def finish(s, carry):
         _, _, to, wanted = r0_plan(s)
-        for k in range(4):
+        for k in range(2):
             sent(s * 6 + k, to[k])
         sent(s * 6 + 4, has_next)
         sent(s * 6 + 5, jnp.where(s == 0, number(core == 0), number(wanted)) == 1)
         sent(50 + s, has_prev)
         _, _, to, wanted = r2_plan(s)
-        for k in range(4):
+        for k in range(2):
             sent(58 + s * 5 + k, to[k])
         sent(62 + s * 5, wanted)
         return carry

time: 48 us -> 46.9 us (0.977)
  Pallas kernels: 47.2 us -> 46.1 us
    pallas_call x1, Pallas kernels: 47.2 us -> 46.1 us  [local(): pl.pallas_call(kernel, out_shape=pltpu.VMEM((BLOCK // HEADS, HEADS * GROU...]
where the time goes in v3:
time: 46.9 us; the launch traced here: 46.8 us
  Pallas kernels  46.1 us (98%)
  local copies, waits for them, and re-layouts  0.71 us (2%)
    pallas_call x1, Pallas kernels, local(): pl.pallas_call(kernel, out_shape=pltpu.VMEM((BLOCK // HEADS, HEADS * GROU...  46.1 us

profile of v3, /device:TPU:30, one launch (start us, length us, event | category | flops | bytes accessed | tf_op | source)
XLA Modules:
  0.0 46.8 jit_solution(7858413162254375944)
XLA Ops:
  0.0 46.1 %attention.1 = bf16[16,8192]{1,0:T(8,128)(2,1)S(1)} custom-call(bf16[128,1024]{1,0:T(8,128)(2,1)} %q_hbm.1, bf16[128,128]{1,0:T(8,128)(2,1)} %k_hbm.1, bf16[128,128]{1,0:T(8,128)(2,1)} %v_hbm.1, s32[1,128]{1,0:T(1,128)} %bitcast.1), custom_call_target="tpu_custom_call" | custom-call | tf_op jit(solution)/shard_map/attention/pallas_call | solution.py:313
  46.1 0.7 %copy.6 = bf16[16,8192]{1,0:T(8,128)(2,1)} copy(bf16[16,8192]{1,0:T(8,128)(2,1)S(1)} %attention.1) | data formatting | bytes 524288

commit v4 on v3

--- a/solution.py
+++ b/solution.py
@@ -133,7 +133,6 @@
     send(own, own + 16, 4, has_next)
     send(own, own + 32, 48, has_next2)
     send(own, sibling, 5, core == 0)
-    send(own, own + WINDOW, 49, far_sender)
     for i in range(1, HEADS):
         other, hd = by_rank(i)
         pl.when(other < rank)(lambda hd=hd: signal(out_sem, own, hd))
@@ -232,13 +231,13 @@
             plan(s)
 
     take((r0, 1), (r0, 2), (r2, 0), (r1, 0))
-    own_step()
-
     def one_step(s, carry):
         pl.when(s == 1)(lambda: take((r0, 3), (r0, 4), (r2, 1), (r2, 2), (r1, 1), (r1, 2)))
+        pl.when(s == 2)(lambda: send(own, own + WINDOW, 49, far_sender))
         pl.when(s == 3)(lambda: take((r0, 5), (r0, 6), (r2, 3), (r2, 4), (r1, 3), (r1, 4)))
-        pl.when(s == 5)(lambda: take((r0, 7), (r2, 5), (r2, 6), (r1, 5), (r1, 6)))
-        pl.when(s == 7)(lambda: take((r2, 7), (r1, 7)))
+        pl.when(s == 5)(lambda: take((r0, 7), (r2, 5), (r1, 5), (r2, 6), (r1, 6)))
+        pl.when(s == 7)(lambda: take((r1, 7), (r2, 7)))
+        pl.when(s == 5)(own_step)
         zz = pick(turns, s)
         in_row = zz < z
         valid = in_row | has_prev2

time: 46.9 us -> 46.2 us (0.985)
  the two profiles are of different devices: /device:TPU:30 before, /device:TPU:62 now
where the time goes in v4:
time: 46.2 us; the launch traced here: 46.1 us
  Pallas kernels  45.4 us (98%)
  local copies, waits for them, and re-layouts  0.71 us (2%)
    pallas_call x1, Pallas kernels, local(): pl.pallas_call(kernel, out_shape=pltpu.VMEM((BLOCK // HEADS, HEADS * GROU...  45.4 us

profile of v4, /device:TPU:62, one launch (start us, length us, event | category | flops | bytes accessed | tf_op | source)
XLA Modules:
  0.0 46.1 jit_solution(10264346233129132998)
XLA Ops:
  0.0 45.4 %attention.1 = bf16[16,8192]{1,0:T(8,128)(2,1)S(1)} custom-call(bf16[128,1024]{1,0:T(8,128)(2,1)} %q_hbm.1, bf16[128,128]{1,0:T(8,128)(2,1)} %k_hbm.1, bf16[128,128]{1,0:T(8,128)(2,1)} %v_hbm.1, s32[1,128]{1,0:T(1,128)} %bitcast.1), custom_call_target="tpu_custom_call" | custom-call | tf_op jit(solution)/shard_map/attention/pallas_call | solution.py:312
  45.4 0.7 %copy.6 = bf16[16,8192]{1,0:T(8,128)(2,1)} copy(bf16[16,8192]{1,0:T(8,128)(2,1)S(1)} %attention.1) | data formatting | bytes 524288

commit v5 on v4

--- a/solution.py
+++ b/solution.py
@@ -233,11 +233,11 @@
     take((r0, 1), (r0, 2), (r2, 0), (r1, 0))
     def one_step(s, carry):
         pl.when(s == 1)(lambda: take((r0, 3), (r0, 4), (r2, 1), (r2, 2), (r1, 1), (r1, 2)))
-        pl.when(s == 2)(lambda: send(own, own + WINDOW, 49, far_sender))
         pl.when(s == 3)(lambda: take((r0, 5), (r0, 6), (r2, 3), (r2, 4), (r1, 3), (r1, 4)))
+        pl.when(s == 3)(lambda: send(own, own + WINDOW, 49, far_sender))
         pl.when(s == 5)(lambda: take((r0, 7), (r2, 5), (r1, 5), (r2, 6), (r1, 6)))
         pl.when(s == 7)(lambda: take((r1, 7), (r2, 7)))
-        pl.when(s == 5)(own_step)
+        pl.when(s == 6)(own_step)
         zz = pick(turns, s)
         in_row = zz < z
         valid = in_row | has_prev2

time: 46.2 us -> 47.4 us (1.026)
  the two profiles are of different devices: /device:TPU:62 before, /device:TPU:30 now
where the time goes in v5:
time: 47.4 us; the launch traced here: 47.2 us
  Pallas kernels  46.5 us (98%)
  local copies, waits for them, and re-layouts  0.71 us (1%)
    pallas_call x1, Pallas kernels, local(): pl.pallas_call(kernel, out_shape=pltpu.VMEM((BLOCK // HEADS, HEADS * GROU...  46.5 us

profile of v5, /device:TPU:30, one launch (start us, length us, event | category | flops | bytes accessed | tf_op | source)
XLA Modules:
  0.0 47.2 jit_solution(13385474972737362970)
XLA Ops:
  0.0 46.5 %attention.1 = bf16[16,8192]{1,0:T(8,128)(2,1)S(1)} custom-call(bf16[128,1024]{1,0:T(8,128)(2,1)} %q_hbm.1, bf16[128,128]{1,0:T(8,128)(2,1)} %k_hbm.1, bf16[128,128]{1,0:T(8,128)(2,1)} %v_hbm.1, s32[1,128]{1,0:T(1,128)} %bitcast.1), custom_call_target="tpu_custom_call" | custom-call | tf_op jit(solution)/shard_map/attention/pallas_call | solution.py:312
  46.5 0.7 %copy.6 = bf16[16,8192]{1,0:T(8,128)(2,1)} copy(bf16[16,8192]{1,0:T(8,128)(2,1)S(1)} %attention.1) | data formatting | bytes 524288
